TPU v7x, 128 devices: a whole 4x4x4 slice. The times are simulated.
128 devices in a mesh: gx: 4 (over x), gy: 32 (over z, y, core).
Axes of the slice: x: 4, y: 4, z: 4, core: 2. Of those that a mesh axis runs over, the one named last changes fastest.
Arguments:
- positions: float32 [8192, 3, 128], P(('gx', 'gy')), may hold values from 0 to 64, as said below
- charges: float32 [8192, 128], P(('gx', 'gy')), may hold values from -8 to 8, as said below
- send_x: int32 [128, 2, 32], P(('gx', 'gy')), may hold values from -1 to 63, as said below
- send_y: int32 [128, 2, 32], P(('gx', 'gy')), may hold values from -1 to 63, as said below
- send_corner: int32 [128, 4, 16], P(('gx', 'gy')), may hold values from -1 to 63, as said below
- near_slot: int32 [8192, 27], P(('gx', 'gy')), may hold values from -1 to 255, as said below
- far_sources: int32 [1024, 316], P(('gx', 'gy')), may hold values from -1 to 1023, as said below
- translations: bfloat16 [121, 38236], replicated, may hold values from -0.0078125 to 0.0078125
Outputs:
- potential: float32 [8192, 128], P(('gx', 'gy'))
- field_strength: float32 [8192, 3, 128], P(('gx', 'gy'))
Inputs may be any that keep to these rules, and one draw needn't show every extreme that they name: `send_x`: row [s, k] lists in increasing order, padded with -1, the local indices of the leaves of device s that hold particles and have local x coordinate 0 (k = 0) or 2 - 1 (k = 1); in every draw some device fills both rows. `send_y`: row [s, k] lists in increasing order, padded with -1, the local indices of the leaves of device s that hold particles and have local y coordinate 0 (k = 0) or 2 - 1 (k = 1); in every draw some device fills both rows. `send_corner`: row [s, k], k = 2 kx + ky, lists in increasing order, padded with -1, the local indices of the leaves of device s that hold particles and have local x coordinate kx (1) and local y coordinate ky (1); in every draw some device fills all four rows. `near_slot`: offset n = 9 (a + 1) + 3 (b + 1) + (c + 1) for the neighbour at (a, b, c) in -1..1; -1 where that leaf lies outside the domain or holds no particles; otherwise the entry of the owner's source table that holds it (n = 13 is the leaf itself). `far_sources`: class k is the k-th offset (a, b, c) in -3..3 with max(|a|, |b|, |c|) > 1, taken in increasing 49 a + 7 b + c; the entry is the upper cell at that offset where it lies in the domain, holds particles and its parent (coordinates halved, rounded down) touches or equals the parent of m, else -1. positions[g, :, p] lies in the unit box of leaf g. `charges`: empty leaves and the slots after each leaf's particle count hold zero.
All inputs are finite; a program needn't handle non-finite values.
Results may differ from a plain program's by a relative error of at most 0.0003.
Values may be sent and summed in bfloat16 or wider, within the bound.
A program may use at most 64 MiB of HBM per device.

v0:
```python
import math

import jax
import jax.numpy as jnp
from jax import lax
from jax.sharding import PartitionSpec as P

ORDER = 10
COEF = 121
BX = 2
BY = 2
BZ = 16
UP_DEV = 8


softening = 0.01


def passed_along(value, axis, steps):
    count = lax.axis_size(axis)
    first, last = (max(0, -steps), min(count, count - steps))
    return lax.ppermute(value, axis, [(source, source + steps) for source in range(first, last)])


def upper_centers(cells, row_count):
    half_y = BY // 2
    half_z = BZ // 2
    device = cells // UP_DEV
    local_ids = cells % UP_DEV
    cell_x = device // row_count * (BX // 2) + local_ids // (half_y * half_z)
    cell_y = device % row_count * half_y + local_ids // half_z % half_y
    cell_z = local_ids % half_z
    return 2.0 * jnp.stack([cell_x, cell_y, cell_z], axis=1).astype(jnp.float32) + 1.0


def harmonics(xcoord, ycoord, zcoord):
    radius_sq = xcoord * xcoord + ycoord * ycoord + zcoord * zcoord
    unity = jnp.ones_like(xcoord)
    nothing = jnp.zeros_like(xcoord)
    solid_harm = {(0, 0): (unity, nothing)}
    for moment in range(1, ORDER + 1):
        real_part, imag_part = solid_harm[moment - 1, moment - 1]
        factor = -0.5 / moment
        solid_harm[moment, moment] = (
            factor * (xcoord * real_part - ycoord * imag_part),
            factor * (xcoord * imag_part + ycoord * real_part),
        )
    for moment in range(ORDER + 1):
        if moment + 1 <= ORDER:
            real_part, imag_part = solid_harm[moment, moment]
            solid_harm[moment + 1, moment] = (zcoord * real_part, zcoord * imag_part)
        for degree in range(moment + 2, ORDER + 1):
            factor = 1.0 / ((degree - moment) * (degree + moment))
            one_back = solid_harm[degree - 1, moment]
            two_back = solid_harm[degree - 2, moment]
            solid_harm[degree, moment] = (
                factor * ((2 * degree - 1) * zcoord * one_back[0] - radius_sq * two_back[0]),
                factor * ((2 * degree - 1) * zcoord * one_back[1] - radius_sq * two_back[1]),
            )
    stacked = []
    for degree in range(ORDER + 1):
        for moment in range(degree + 1):
            scaling = math.sqrt(math.factorial(degree + moment) * math.factorial(degree - moment))
            real_part, imag_part = solid_harm[degree, moment]
            stacked.append(scaling * real_part)
            if moment > 0:
                stacked.append(scaling * imag_part)
    return jnp.stack(stacked, axis=0)


def leaf_multipoles(positions, charges, centers):
    repeated = jnp.repeat(centers, 8, axis=0)
    offsets = positions - repeated[:, :, None]
    harm = harmonics(offsets[:, 0], offsets[:, 1], offsets[:, 2])
    per_leaf = jnp.sum(harm * charges[None], axis=2)
    return per_leaf.reshape(COEF, -1, 8).sum(axis=2)


def far_field(positions, centers, local_exp):
    repeated = jnp.repeat(centers, 8, axis=0)
    per_leaf = jnp.repeat(local_exp, 8, axis=1)

    def summed_field(points):
        offsets = points - repeated[:, :, None]
        harm = harmonics(offsets[:, 0], offsets[:, 1], offsets[:, 2])
        return jnp.sum(harm * per_leaf[:, :, None], axis=0)

    potential, pullback = jax.vjp(summed_field, positions)
    gradient = pullback(jnp.ones_like(potential))[0]
    return (potential, -gradient)


def translate(everyone, far_sources, translations):
    usable = far_sources >= 0
    picked = jnp.take(everyone, jnp.maximum(far_sources, 0), axis=1)
    picked = jnp.where(usable[None], picked, jnp.zeros((), picked.dtype))
    stacked = jnp.transpose(picked, (1, 2, 0)).reshape(picked.shape[1], -1)
    return jnp.einsum("uk,ik->iu", stacked, translations, preferred_element_type=jnp.float32)


def near_field(targets, source_points, source_charge, slot_ids):
    identity = jnp.eye(targets.shape[2], dtype=jnp.float32)

    def neighbour_step(running, inputs):
        potential, electric = running
        column, neighbour = inputs
        present = column >= 0
        safe = jnp.maximum(column, 0)
        points = source_points[safe]
        charge = jnp.where(present[:, None], source_charge[safe], 0.0)
        separation = targets[:, :, :, None] - points[:, :, None, :]
        distance = jnp.sum(separation * separation, axis=1) + softening
        inverse = lax.rsqrt(distance)
        self_mask = jnp.where(neighbour == 13, 1.0 - identity, 1.0)
        weight = charge[:, None, :] * inverse * self_mask
        potential = potential + jnp.sum(weight, axis=2)
        electric = electric + jnp.sum(separation * (weight * inverse * inverse)[:, None], axis=3)
        return ((potential, electric), None)

    start = (
        jnp.zeros(targets.shape[:1] + targets.shape[2:], jnp.float32),
        jnp.zeros(targets.shape, jnp.float32),
    )
    result = lax.scan(neighbour_step, start, (slot_ids.T, jnp.arange(27, dtype=jnp.int32)))[0]
    return result


def pack_blocks(listing, positions, charges):
    present = listing >= 0
    chosen = jnp.maximum(listing, 0)
    points = jnp.where(present[:, :, None, None], positions[chosen], 0.0)
    charge = jnp.where(present[:, :, None], charges[chosen], 0.0)
    return jnp.concatenate([points, charge[:, :, None]], axis=2)


def per_device(
    positions, charges, send_x, send_y, send_corner, near_slot, far_sources, translations
):
    inner_count = lax.axis_size("gy")
    device = lax.axis_index("gx") * inner_count + lax.axis_index("gy")
    cells = device * UP_DEV + jnp.arange(UP_DEV, dtype=jnp.int32)
    centers = upper_centers(cells, inner_count)
    multipole = leaf_multipoles(positions, charges, centers).astype(jnp.bfloat16)
    everyone = lax.all_gather(multipole, ("gx", "gy"), axis=1, tiled=True)
    local_exp = translate(everyone, far_sources, translations)
    far_pot, far_force = far_field(positions, centers, local_exp)
    own_blocks = jnp.concatenate([positions, charges[:, None]], axis=1)
    packed_x = pack_blocks(send_x[0], positions, charges)
    packed_y = pack_blocks(send_y[0], positions, charges)
    packed_edge = pack_blocks(send_corner[0], positions, charges)
    table_parts = [own_blocks]
    for block in range(2):
        table_parts.append(passed_along(packed_x[1 - block], "gx", 1 - 2 * block))
    for block in range(2):
        table_parts.append(passed_along(packed_y[1 - block], "gy", 1 - 2 * block))
    for block in range(4):
        step_x = 2 * (block // 2) - 1
        step_y = 2 * (block % 2) - 1
        table_parts.append(
            passed_along(packed_edge[3 - block], ("gx", "gy"), -(step_x * inner_count + step_y))
        )
    table = jnp.concatenate(table_parts, axis=0)
    near_pot, near_force = near_field(positions, table[:, :3], table[:, 3], near_slot)
    return (far_pot + near_pot, far_force + near_force)


def solution(mesh):
    return jax.shard_map(
        per_device,
        mesh=mesh,
        in_specs=(
            P(("gx", "gy"), None, None),
            P(("gx", "gy"), None),
            P(("gx", "gy"), None, None),
            P(("gx", "gy"), None, None),
            P(("gx", "gy"), None, None),
            P(("gx", "gy"), None),
            P(("gx", "gy"), None),
            P(),
        ),
        out_specs=(P(("gx", "gy"), None), P(("gx", "gy"), None, None)),
        check_vma=False,
    )
```

profile of v0, /device:TPU:69, one launch (start us, length us, event | category | flops | bytes accessed | tf_op | source)
XLA Modules:
  0.0 861.4 jit_solution(16908647988988412900)
XLA Ops:
  108.7 34.7 %all_gather.3 = bf16[121,1024]{0,1:T(8,128)(2,1)S(1)} all-gather(bf16[121,8]{0,1:T(8,128)(2,1)S(1)} %bitcast_reduce_fusion), channel_id=1, replica_groups=mesh['gx'=4,'gy'=32] {'gx','gy'}, dimensions={1}, use_global_device_ids=true | all-gather | bytes 249744 | tf_op jit(solution)/shard_map/all_gather | solution.py:144
  204.9 655.2 %while.13 = (s32[]{:T(128)}, f32[64,128]{1,0:T(8,128)S(1)}, f32[64,3,128]{2,1,0:T(4,128)S(1)}, s32[27,64]{1,0:T(8,128)}, f32[256,128]{1,0:T(8,128)S(1)}, /*index...) while((s32[]{:T(128)}, f32[64,128]{1,0:T(8,128)S(1)}, ...), condition=%wide.region_7.8_spmd.clone, body=%wide.region_3.7_spmd.clone.sunk | while | flops 24224900 | bytes 18192156 | solution.py:124
  220.2 8.9 %fusion.455 = f32[64,3,128]{2,1,0:T(4,128)S(1)} fusion(f32[64,128,128]{2,1,0:T(8,128)} %get-tuple-element.385, f32[64,3,128]{2,1,0:T(4,128)S(1)} %gather_fusion, f32[64,3,128]{2,1,0:T(4,128)S(1)} %get-tuple-element.413), kind=kLoop, calls=%fused_computation.13.clone.1 | loop fusion | flops 9412608 | bytes 4489216 | tf_op jit(solution)/shard_map/while/body/eval_jaxpr/reduce_sum | solution.py:117
  268.7 8.9 %fusion.455 = f32[64,3,128]{2,1,0:T(4,128)S(1)} fusion(f32[64,128,128]{2,1,0:T(8,128)} %get-tuple-element.385, f32[64,3,128]{2,1,0:T(4,128)S(1)} %gather_fusion, f32[64,3,128]{2,1,0:T(4,128)S(1)} %get-tuple-element.413), kind=kLoop, calls=%fused_computation.13.clone.1 | loop fusion | flops 9412608 | bytes 4489216 | tf_op jit(solution)/shard_map/while/body/eval_jaxpr/reduce_sum | solution.py:117
  293.0 8.9 %fusion.455 = f32[64,3,128]{2,1,0:T(4,128)S(1)} fusion(f32[64,128,128]{2,1,0:T(8,128)} %get-tuple-element.385, f32[64,3,128]{2,1,0:T(4,128)S(1)} %gather_fusion, f32[64,3,128]{2,1,0:T(4,128)S(1)} %get-tuple-element.413), kind=kLoop, calls=%fused_computation.13.clone.1 | loop fusion | flops 9412608 | bytes 4489216 | tf_op jit(solution)/shard_map/while/body/eval_jaxpr/reduce_sum | solution.py:117
  317.2 8.9 %fusion.455 = f32[64,3,128]{2,1,0:T(4,128)S(1)} fusion(f32[64,128,128]{2,1,0:T(8,128)} %get-tuple-element.385, f32[64,3,128]{2,1,0:T(4,128)S(1)} %gather_fusion, f32[64,3,128]{2,1,0:T(4,128)S(1)} %get-tuple-element.413), kind=kLoop, calls=%fused_computation.13.clone.1 | loop fusion | flops 9412608 | bytes 4489216 | tf_op jit(solution)/shard_map/while/body/eval_jaxpr/reduce_sum | solution.py:117
  365.7 8.9 %fusion.455 = f32[64,3,128]{2,1,0:T(4,128)S(1)} fusion(f32[64,128,128]{2,1,0:T(8,128)} %get-tuple-element.385, f32[64,3,128]{2,1,0:T(4,128)S(1)} %gather_fusion, f32[64,3,128]{2,1,0:T(4,128)S(1)} %get-tuple-element.413), kind=kLoop, calls=%fused_computation.13.clone.1 | loop fusion | flops 9412608 | bytes 4489216 | tf_op jit(solution)/shard_map/while/body/eval_jaxpr/reduce_sum | solution.py:117
  390.0 8.9 %fusion.455 = f32[64,3,128]{2,1,0:T(4,128)S(1)} fusion(f32[64,128,128]{2,1,0:T(8,128)} %get-tuple-element.385, f32[64,3,128]{2,1,0:T(4,128)S(1)} %gather_fusion, f32[64,3,128]{2,1,0:T(4,128)S(1)} %get-tuple-element.413), kind=kLoop, calls=%fused_computation.13.clone.1 | loop fusion | flops 9412608 | bytes 4489216 | tf_op jit(solution)/shard_map/while/body/eval_jaxpr/reduce_sum | solution.py:117
  414.3 8.9 %fusion.455 = f32[64,3,128]{2,1,0:T(4,128)S(1)} fusion(f32[64,128,128]{2,1,0:T(8,128)} %get-tuple-element.385, f32[64,3,128]{2,1,0:T(4,128)S(1)} %gather_fusion, f32[64,3,128]{2,1,0:T(4,128)S(1)} %get-tuple-element.413), kind=kLoop, calls=%fused_computation.13.clone.1 | loop fusion | flops 9412608 | bytes 4489216 | tf_op jit(solution)/shard_map/while/body/eval_jaxpr/reduce_sum | solution.py:117
  438.6 8.9 %fusion.455 = f32[64,3,128]{2,1,0:T(4,128)S(1)} fusion(f32[64,128,128]{2,1,0:T(8,128)} %get-tuple-element.385, f32[64,3,128]{2,1,0:T(4,128)S(1)} %gather_fusion, f32[64,3,128]{2,1,0:T(4,128)S(1)} %get-tuple-element.413), kind=kLoop, calls=%fused_computation.13.clone.1 | loop fusion | flops 9412608 | bytes 4489216 | tf_op jit(solution)/shard_map/while/body/eval_jaxpr/reduce_sum | solution.py:117
  462.8 8.9 %fusion.455 = f32[64,3,128]{2,1,0:T(4,128)S(1)} fusion(f32[64,128,128]{2,1,0:T(8,128)} %get-tuple-element.385, f32[64,3,128]{2,1,0:T(4,128)S(1)} %gather_fusion, f32[64,3,128]{2,1,0:T(4,128)S(1)} %get-tuple-element.413), kind=kLoop, calls=%fused_computation.13.clone.1 | loop fusion | flops 9412608 | bytes 4489216 | tf_op jit(solution)/shard_map/while/body/eval_jaxpr/reduce_sum | solution.py:117
  487.1 8.9 %fusion.455 = f32[64,3,128]{2,1,0:T(4,128)S(1)} fusion(f32[64,128,128]{2,1,0:T(8,128)} %get-tuple-element.385, f32[64,3,128]{2,1,0:T(4,128)S(1)} %gather_fusion, f32[64,3,128]{2,1,0:T(4,128)S(1)} %get-tuple-element.413), kind=kLoop, calls=%fused_computation.13.clone.1 | loop fusion | flops 9412608 | bytes 4489216 | tf_op jit(solution)/shard_map/while/body/eval_jaxpr/reduce_sum | solution.py:117
  511.3 8.9 %fusion.455 = f32[64,3,128]{2,1,0:T(4,128)S(1)} fusion(f32[64,128,128]{2,1,0:T(8,128)} %get-tuple-element.385, f32[64,3,128]{2,1,0:T(4,128)S(1)} %gather_fusion, f32[64,3,128]{2,1,0:T(4,128)S(1)} %get-tuple-element.413), kind=kLoop, calls=%fused_computation.13.clone.1 | loop fusion | flops 9412608 | bytes 4489216 | tf_op jit(solution)/shard_map/while/body/eval_jaxpr/reduce_sum | solution.py:117
  535.6 8.9 %fusion.455 = f32[64,3,128]{2,1,0:T(4,128)S(1)} fusion(f32[64,128,128]{2,1,0:T(8,128)} %get-tuple-element.385, f32[64,3,128]{2,1,0:T(4,128)S(1)} %gather_fusion, f32[64,3,128]{2,1,0:T(4,128)S(1)} %get-tuple-element.413), kind=kLoop, calls=%fused_computation.13.clone.1 | loop fusion | flops 9412608 | bytes 4489216 | tf_op jit(solution)/shard_map/while/body/eval_jaxpr/reduce_sum | solution.py:117
  559.9 8.9 %fusion.455 = f32[64,3,128]{2,1,0:T(4,128)S(1)} fusion(f32[64,128,128]{2,1,0:T(8,128)} %get-tuple-element.385, f32[64,3,128]{2,1,0:T(4,128)S(1)} %gather_fusion, f32[64,3,128]{2,1,0:T(4,128)S(1)} %get-tuple-element.413), kind=kLoop, calls=%fused_computation.13.clone.1 | loop fusion | flops 9412608 | bytes 4489216 | tf_op jit(solution)/shard_map/while/body/eval_jaxpr/reduce_sum | solution.py:117
  584.1 8.9 %fusion.455 = f32[64,3,128]{2,1,0:T(4,128)S(1)} fusion(f32[64,128,128]{2,1,0:T(8,128)} %get-tuple-element.385, f32[64,3,128]{2,1,0:T(4,128)S(1)} %gather_fusion, f32[64,3,128]{2,1,0:T(4,128)S(1)} %get-tuple-element.413), kind=kLoop, calls=%fused_computation.13.clone.1 | loop fusion | flops 9412608 | bytes 4489216 | tf_op jit(solution)/shard_map/while/body/eval_jaxpr/reduce_sum | solution.py:117
  608.4 8.9 %fusion.455 = f32[64,3,128]{2,1,0:T(4,128)S(1)} fusion(f32[64,128,128]{2,1,0:T(8,128)} %get-tuple-element.385, f32[64,3,128]{2,1,0:T(4,128)S(1)} %gather_fusion, f32[64,3,128]{2,1,0:T(4,128)S(1)} %get-tuple-element.413), kind=kLoop, calls=%fused_computation.13.clone.1 | loop fusion | flops 9412608 | bytes 4489216 | tf_op jit(solution)/shard_map/while/body/eval_jaxpr/reduce_sum | solution.py:117
  632.7 8.9 %fusion.455 = f32[64,3,128]{2,1,0:T(4,128)S(1)} fusion(f32[64,128,128]{2,1,0:T(8,128)} %get-tuple-element.385, f32[64,3,128]{2,1,0:T(4,128)S(1)} %gather_fusion, f32[64,3,128]{2,1,0:T(4,128)S(1)} %get-tuple-element.413), kind=kLoop, calls=%fused_computation.13.clone.1 | loop fusion | flops 9412608 | bytes 4489216 | tf_op jit(solution)/shard_map/while/body/eval_jaxpr/reduce_sum | solution.py:117
  681.2 8.9 %fusion.455 = f32[64,3,128]{2,1,0:T(4,128)S(1)} fusion(f32[64,128,128]{2,1,0:T(8,128)} %get-tuple-element.385, f32[64,3,128]{2,1,0:T(4,128)S(1)} %gather_fusion, f32[64,3,128]{2,1,0:T(4,128)S(1)} %get-tuple-element.413), kind=kLoop, calls=%fused_computation.13.clone.1 | loop fusion | flops 9412608 | bytes 4489216 | tf_op jit(solution)/shard_map/while/body/eval_jaxpr/reduce_sum | solution.py:117
  729.7 8.9 %fusion.455 = f32[64,3,128]{2,1,0:T(4,128)S(1)} fusion(f32[64,128,128]{2,1,0:T(8,128)} %get-tuple-element.385, f32[64,3,128]{2,1,0:T(4,128)S(1)} %gather_fusion, f32[64,3,128]{2,1,0:T(4,128)S(1)} %get-tuple-element.413), kind=kLoop, calls=%fused_computation.13.clone.1 | loop fusion | flops 9412608 | bytes 4489216 | tf_op jit(solution)/shard_map/while/body/eval_jaxpr/reduce_sum | solution.py:117
  754.0 8.9 %fusion.455 = f32[64,3,128]{2,1,0:T(4,128)S(1)} fusion(f32[64,128,128]{2,1,0:T(8,128)} %get-tuple-element.385, f32[64,3,128]{2,1,0:T(4,128)S(1)} %gather_fusion, f32[64,3,128]{2,1,0:T(4,128)S(1)} %get-tuple-element.413), kind=kLoop, calls=%fused_computation.13.clone.1 | loop fusion | flops 9412608 | bytes 4489216 | tf_op jit(solution)/shard_map/while/body/eval_jaxpr/reduce_sum | solution.py:117
  802.5 8.9 %fusion.455 = f32[64,3,128]{2,1,0:T(4,128)S(1)} fusion(f32[64,128,128]{2,1,0:T(8,128)} %get-tuple-element.385, f32[64,3,128]{2,1,0:T(4,128)S(1)} %gather_fusion, f32[64,3,128]{2,1,0:T(4,128)S(1)} %get-tuple-element.413), kind=kLoop, calls=%fused_computation.13.clone.1 | loop fusion | flops 9412608 | bytes 4489216 | tf_op jit(solution)/shard_map/while/body/eval_jaxpr/reduce_sum | solution.py:117
  826.8 8.9 %fusion.455 = f32[64,3,128]{2,1,0:T(4,128)S(1)} fusion(f32[64,128,128]{2,1,0:T(8,128)} %get-tuple-element.385, f32[64,3,128]{2,1,0:T(4,128)S(1)} %gather_fusion, f32[64,3,128]{2,1,0:T(4,128)S(1)} %get-tuple-element.413), kind=kLoop, calls=%fused_computation.13.clone.1 | loop fusion | flops 9412608 | bytes 4489216 | tf_op jit(solution)/shard_map/while/body/eval_jaxpr/reduce_sum | solution.py:117
  851.1 8.9 %fusion.455 = f32[64,3,128]{2,1,0:T(4,128)S(1)} fusion(f32[64,128,128]{2,1,0:T(8,128)} %get-tuple-element.385, f32[64,3,128]{2,1,0:T(4,128)S(1)} %gather_fusion, f32[64,3,128]{2,1,0:T(4,128)S(1)} %get-tuple-element.413), kind=kLoop, calls=%fused_computation.13.clone.1 | loop fusion | flops 9412608 | bytes 4489216 | tf_op jit(solution)/shard_map/while/body/eval_jaxpr/reduce_sum | solution.py:117
  (880 shorter events, 611.7 us)
Async XLA Ops:
  0.6 22.0 %copy-start.1 = (f32[64,128]{1,0:T(8,128)S(1)}, f32[64,128]{1,0:T(8,128)}, u32[]{:S(2)}) copy-start(f32[64,128]{1,0:T(8,128)} %param.11) | copy-start | bytes 98308
  0.6 22.6 %copy-start = (f32[64,3,128]{2,0,1:T(8,128)S(1)}, f32[64,3,128]{2,0,1:T(8,128)}, u32[]{:S(2)}) copy-start(f32[64,3,128]{2,0,1:T(8,128)} %param.10) | copy-start | bytes 294916
  0.7 21.9 %copy-start.5 = (s32[1,4,16]{2,1,0:T(4,128)S(1)}, s32[1,4,16]{2,1,0:T(4,128)}, u32[]{:S(2)}) copy-start(s32[1,4,16]{2,1,0:T(4,128)} %param.14) | copy-start | bytes 772
  0.7 29.1 %copy-start.2 = (s32[8,316]{1,0:T(8,128)S(1)}, s32[8,316]{1,0:T(8,128)}, u32[]{:S(2)}) copy-start(s32[8,316]{1,0:T(8,128)} %param.16) | copy-start | bytes 30340
  5.5 186.6 %collective-permute-start = (f32[32,4,128]{2,1,0:T(4,128)S(1)}, f32[32,4,128]{2,1,0:T(4,128)S(1)}, u32[]{:S(2)}, u32[]{:S(2)}) collective-permute-start(f32[32,4,128]{2,1,0:T(4,128)S(1)} %get-tuple-element.310), channel_id=1, source_target_pairs={{0,32},{32,64},{64,96},{1,33},{33,65},{65,97},{2,34},{34,66},{66,9... | collective-permute-start | bytes 196616 | tf_op jit(solution)/shard_map/ppermute | solution.py:22
  8.3 186.4 %collective-permute-start.1 = (f32[32,4,128]{2,1,0:T(4,128)S(1)}, f32[32,4,128]{2,1,0:T(4,128)S(1)}, u32[]{:S(2)}, u32[]{:S(2)}) collective-permute-start(f32[32,4,128]{2,1,0:T(4,128)S(1)} %get-tuple-element.309), channel_id=1, source_target_pairs={{32,0},{64,32},{96,64},{33,1},{65,33},{97,65},{34,2},{66,34},{98,6... | collective-permute-start | bytes 196616 | tf_op jit(solution)/shard_map/ppermute | solution.py:22
  16.3 182.3 %collective-permute-start.2 = (f32[32,4,128]{2,1,0:T(4,128)S(1)}, f32[32,4,128]{2,1,0:T(4,128)S(1)}, u32[]{:S(2)}, u32[]{:S(2)}) collective-permute-start(f32[32,4,128]{2,1,0:T(4,128)S(1)} %get-tuple-element.308), channel_id=1, source_target_pairs={{0,1},{1,2},{2,3},{3,4},{4,5},{5,6},{6,7},{7,8},{8,9},{9,10},{10,1... | collective-permute-start | bytes 196616 | tf_op jit(solution)/shard_map/ppermute | solution.py:22
  20.6 180.0 %collective-permute-start.3 = (f32[32,4,128]{2,1,0:T(4,128)S(1)}, f32[32,4,128]{2,1,0:T(4,128)S(1)}, u32[]{:S(2)}, u32[]{:S(2)}) collective-permute-start(f32[32,4,128]{2,1,0:T(4,128)S(1)} %get-tuple-element.307), channel_id=1, source_target_pairs={{1,0},{2,1},{3,2},{4,3},{5,4},{6,5},{7,6},{8,7},{9,8},{10,9},{11,1... | collective-permute-start | bytes 196616 | tf_op jit(solution)/shard_map/ppermute | solution.py:22
  24.9 175.8 %collective-permute-start.4 = (f32[16,4,128]{2,1,0:T(4,128)}, f32[16,4,128]{2,1,0:T(4,128)}, u32[]{:S(2)}, u32[]{:S(2)}) collective-permute-start(f32[16,4,128]{2,1,0:T(4,128)} %get-tuple-element.304), channel_id=1, source_target_pairs={{0,33},{1,34},{2,35},{3,36},{4,37},{5,38},{6,39},{7,40},{8,41},{9,... | collective-permute-start | bytes 98312 | tf_op jit(solution)/shard_map/ppermute | solution.py:22
  155.4 36.6 %copy-start.4 = (f32[16,4,128]{2,1,0:T(4,128)S(1)}, f32[16,4,128]{2,1,0:T(4,128)}, u32[]{:S(2)}) copy-start(f32[16,4,128]{2,1,0:T(4,128)} %get-tuple-element.305) | copy-start | bytes 98308
  156.0 38.7 %copy-start.3 = (f32[16,4,128]{2,1,0:T(4,128)S(1)}, f32[16,4,128]{2,1,0:T(4,128)}, u32[]{:S(2)}) copy-start(f32[16,4,128]{2,1,0:T(4,128)} %get-tuple-element.306) | copy-start | bytes 98308
  192.1 9.4 %collective-permute-start.5 = (f32[16,4,128]{2,1,0:T(4,128)S(1)}, f32[16,4,128]{2,1,0:T(4,128)S(1)}, u32[]{:S(2)}, u32[]{:S(2)}) collective-permute-start(f32[16,4,128]{2,1,0:T(4,128)S(1)} %copy-done.4), channel_id=1, source_target_pairs={{0,31},{1,32},{2,33},{3,34},{4,35},{5,36},{6,37},{7,38},{8,39},{9,... | collective-permute-start | bytes 98312 | tf_op jit(solution)/shard_map/ppermute | solution.py:22
  194.7 6.8 collective-permute-start.6
  198.6 6.1 collective-permute-start.7
where the time goes:
time: 875 us; the launch traced here: 861 us
  other arithmetic  685 us (78%)
  local copies, waits for them, and re-layouts  89.5 us (10%)
  blocking collectives  34.7 us (4%)
  starting transfers between devices  24.2 us (3%)
  loops' own time  18.4 us (2%)
    reduce_sum x27, other arithmetic, neighbour_step(): jnp.sum(separation * (weight * inverse * inverse)[:, None], axis=3)  239 us
    reduce_sum x27, other arithmetic, neighbour_step(): distance = jnp.sum(separation * separation, axis=1) + softening  163 us
    mul x27, other arithmetic, neighbour_step(): weight * inverse * inverse  140 us
    unnamed x121, other arithmetic  73.9 us
    all_gather x1, blocking collectives, per_device(): everyone = lax.all_gather(multipole, ('gx', 'gy'), axis=1, tiled=True)  34.7 us
    ppermute x8, starting transfers between devices, passed_along(): lax.ppermute(value, axis, [(source, source + steps) for source in range(f...  24.2 us
    max x27, other arithmetic, neighbour_step(): safe = jnp.maximum(column, 0)  18.8 us
    ge x27, other arithmetic, neighbour_step(): present = column >= 0  18.8 us
  transfers between devices with their start and end apart: 8, of which 1 were waited for; matrix products, arithmetic and copies ran while one was open for 16% of the time, Pallas kernels for 0%

commit v1 on v0

v1 whole, which is shorter than its diff:
```python
import math

import jax
import jax.numpy as jnp
from jax import lax
from jax.experimental import pallas as pl
from jax.experimental.pallas import tpu as pltpu
from jax.sharding import PartitionSpec as P

ORDER = 10
COEF = 121
CLASSES = 316
SOFTENING = 0.01
GX = 4
GY = 32
REACH = 3
WIDTH = 2 * REACH + 1
SLOTS = WIDTH * WIDTH
OWN = SLOTS // 2
TILES = 299
MESH = pl.DeviceIdType.MESH

far_offsets = [
    (a, b, c)
    for a in range(-3, 4)
    for b in range(-3, 4)
    for c in range(-3, 4)
    if max(abs(a), abs(b), abs(c)) > 1
]


def scale_of(degree, moment):
    return math.sqrt(math.factorial(degree + moment) * math.factorial(degree - moment))


def coef_index(degree, moment, imag=0):
    return degree * degree + (2 * moment - 1 + imag if moment else 0)


def harmonic_columns(x, y, z, order):
    radius_sq = x * x + y * y + z * z
    diag = (jnp.ones_like(x), None)
    for moment in range(order + 1):
        if moment == 1:
            diag = (-0.5 * x, -0.5 * y)
        elif moment > 1:
            factor = -0.5 / moment
            real, imag = diag
            diag = (factor * (x * real - y * imag), factor * (x * imag + y * real))
        yield moment, moment, diag[0], diag[1]
        two_back, one_back = None, diag
        for degree in range(moment + 1, order + 1):
            if degree == moment + 1:
                step = tuple(None if v is None else z * v for v in one_back)
            else:
                factor = 1.0 / ((degree - moment) * (degree + moment))
                zf = (factor * (2 * degree - 1)) * z
                rf = factor * radius_sq
                step = tuple(
                    None if v is None else zf * v - rf * w for v, w in zip(one_back, two_back)
                )
            yield degree, moment, step[0], step[1]
            two_back, one_back = one_back, step


def partners(i, j, t):
    pi = t // 6
    pj = (j // 2) * 2 - 2 + t % 6
    ok = (pj >= 0) & (pj < GY) & ((pi != i) | (pj != j))
    return pi, pj, ok


halo_moves = (
    [((1, 0), 9 + y, 1 + y) for y in range(2)]
    + [((-1, 0), 5 + y, 13 + y) for y in range(2)]
    + [((0, 1), 4 * x + 2, 4 * x) for x in (1, 2)]
    + [((0, -1), 4 * x + 1, 4 * x + 3) for x in (1, 2)]
    + [((1, 1), 10, 0), ((1, -1), 9, 3), ((-1, 1), 6, 12), ((-1, -1), 5, 15)]
)


def exchange_kernel(pos_ref, charge_ref, tab, mg, cnt, send_m, recv_m, send_h, recv_h):
    i = lax.axis_index("gx")
    j = lax.axis_index("gy")
    zero_tile = jnp.zeros((8, 128), jnp.float32)
    mg[...] = jnp.zeros(mg.shape, jnp.float32)
    for column in range(16):
        if column not in (5, 6, 9, 10):
            tab[column] = jnp.zeros(tab.shape[1:], jnp.float32)

    barrier = pltpu.get_barrier_semaphore()

    def signal_partner(t, count):
        pi, pj, ok = partners(i, j, t)

        @pl.when(ok)
        def _():
            pl.semaphore_signal(barrier, inc=1, device_id=(pi, pj), device_id_type=MESH)

        return count + ok.astype(jnp.int32)

    total = lax.fori_loop(0, 24, signal_partner, jnp.int32(0))
    for bx in range(2):
        for by in range(2):
            column = 4 * (1 + bx) + 1 + by
            for bz in range(2):
                rows = pl.ds(bx + 2 * by + 4 * bz, 8, stride=8)
                dest = pl.ds(bz, 8, stride=2)
                for comp in range(3):
                    tab[column, comp, dest, :] = pos_ref[comp, rows, :]
                tab[column, 3, dest, :] = charge_ref[rows, :]
    pl.semaphore_wait(barrier, total)

    def halo_copy(move, index):
        (da, db), source, dest = move
        return pltpu.make_async_remote_copy(
            src_ref=tab.at[source],
            dst_ref=tab.at[dest],
            send_sem=send_h.at[index],
            recv_sem=recv_h.at[index],
            device_id=(i + da, j + db),
            device_id_type=MESH,
        )

    def inside(a, b):
        return (i + a >= 0) & (i + a < GX) & (j + b >= 0) & (j + b < GY)

    for index, move in enumerate(halo_moves):

        @pl.when(inside(*move[0]))
        def _():
            halo_copy(move, index).start()

    cell = lax.broadcasted_iota(jnp.int32, (8, 128), 0).astype(jnp.float32)
    lane = lax.broadcasted_iota(jnp.int32, (8, 128), 1)
    stacked = [
        jnp.stack([pos_ref[comp, pl.ds(b, 8, stride=8), :] for b in range(8)]) for comp in range(3)
    ]
    charge = jnp.stack([charge_ref[pl.ds(b, 8, stride=8), :] for b in range(8)])
    x = stacked[0] - (2 * i + 1).astype(jnp.float32)
    y = stacked[1] - (2 * j + 1).astype(jnp.float32)
    z = stacked[2] - (2.0 * cell + 1.0)[None]
    moments = zero_tile
    for degree, moment, real, imag in harmonic_columns(x, y, z, ORDER):
        for part, value in enumerate((real, imag)):
            if value is None:
                continue
            summed = jnp.sum(jnp.sum(value * charge, axis=0), axis=1, keepdims=True)
            index = coef_index(degree, moment, part)
            moments = jnp.where(lane == index, scale_of(degree, moment) * summed, moments)
    mg[OWN] = moments.astype(jnp.bfloat16).astype(jnp.float32)

    def multipole_copy(pi, pj):
        there = (i - pi + REACH) * WIDTH + (j - pj + REACH)
        return pltpu.make_async_remote_copy(
            src_ref=mg.at[OWN],
            dst_ref=mg.at[there],
            send_sem=send_m.at[there],
            recv_sem=recv_m.at[there],
            device_id=(pi, pj),
            device_id_type=MESH,
        )

    def send_multipole(t, carry):
        pi, pj, ok = partners(i, j, t)

        @pl.when(ok)
        def _():
            multipole_copy(pi, pj).start()

        return carry

    lax.fori_loop(0, 24, send_multipole, 0)

    def wait_multipole(t, carry):
        pi, pj, ok = partners(i, j, t)

        @pl.when(ok)
        def _():
            multipole_copy(pi, pj).wait_send()
            here = (pi - i + REACH) * WIDTH + (pj - j + REACH)
            pltpu.make_async_remote_copy(
                src_ref=mg.at[OWN],
                dst_ref=mg.at[here],
                send_sem=send_m.at[here],
                recv_sem=recv_m.at[here],
                device_id=(pi, pj),
                device_id_type=MESH,
            ).wait_recv()

        return carry

    lax.fori_loop(0, 24, wait_multipole, 0)
    for index, move in enumerate(halo_moves):
        da, db = move[0]

        @pl.when(inside(da, db))
        def _():
            halo_copy(move, index).wait_send()

        @pl.when(inside(-da, -db))
        def _():
            halo_copy(move, index).wait_recv()

    counts = jnp.zeros((16, 128), jnp.int32)
    lanes = lax.broadcasted_iota(jnp.int32, (16, 128), 1)
    for column in range(16):
        used = jnp.where(tab[column, 3] != 0.0, lanes + 1, 0)
        counts = jnp.where(lanes == column, jnp.max(used, axis=1, keepdims=True), counts)
    cnt[...] = counts


def exchange(pos, charges):
    vmem = pl.BlockSpec(memory_space=pltpu.VMEM)
    return pl.pallas_call(
        exchange_kernel,
        out_shape=(
            jax.ShapeDtypeStruct((16, 4, 16, 128), jnp.float32),
            jax.ShapeDtypeStruct((SLOTS, 8, 128), jnp.float32),
            jax.ShapeDtypeStruct((16, 128), jnp.int32),
        ),
        in_specs=[vmem, vmem],
        out_specs=(vmem, vmem, vmem),
        scratch_shapes=[
            pltpu.SemaphoreType.DMA((SLOTS,)),
            pltpu.SemaphoreType.DMA((SLOTS,)),
            pltpu.SemaphoreType.DMA((len(halo_moves),)),
            pltpu.SemaphoreType.DMA((len(halo_moves),)),
        ],
        compiler_params=pltpu.CompilerParams(
            collective_id=0, has_side_effects=True, vmem_limit_bytes=40 << 20
        ),
        name="exchange",
    )(pos, charges)


source_lists = [
    ((5, 6, 9, 10), (5, 6, 9, 10)),
    ((1, 2), (5, 6)),
    ((13, 14), (9, 10)),
    ((4, 8), (5, 9)),
    ((7, 11), (6, 10)),
    ((0,), (5,)),
    ((3,), (6,)),
    ((12,), (9,)),
    ((15,), (10,)),
]
own_columns = (5, 6, 9, 10)
unrolls = {4: 4, 2: 8, 1: 8}
list_rows = [(len(sources) * 16 + 1) * 128 for sources, _ in source_lists]
list_base = [sum(list_rows[:n]) for n in range(len(list_rows))]
TABLE_ROWS = sum(list_rows)


def build_sources(tab, cnt, columns, table, starts):
    for column in range(16):
        flat = tab[column].reshape(64, 128)
        columns[column] = jnp.transpose(jnp.concatenate([flat, flat], axis=0))

    def step(z, offsets):
        offsets = list(offsets)
        for n, (sources, _) in enumerate(source_lists):
            starts[n, z] = offsets[n]
            for column in sources:
                rows = pl.ds(pl.multiple_of(list_base[n] + offsets[n] * 8, 8), 128)
                table[rows, :] = pltpu.roll(columns[column], (128 - z) % 128, 1)
                offsets[n] = offsets[n] + (cnt[z, column] + 7) // 8
        return tuple(offsets)

    ends = lax.fori_loop(0, 16, step, (jnp.int32(0),) * len(source_lists))
    for n, end in enumerate(ends):
        starts[n, 16] = end
        rows = pl.ds(pl.multiple_of(list_base[n] + end * 8, 8), 128)
        table[rows, :] = jnp.zeros((128, 128), jnp.float32)


def near_field(tab, table, starts, near):
    def step(z, carry):
        for n, (_, targets) in enumerate(source_lists):
            unroll = unrolls[len(targets)]
            first = starts[n, jnp.maximum(z - 1, 0)]
            last = starts[n, jnp.minimum(z + 2, 16)]
            at = [
                [jnp.broadcast_to(tab[t, comp, pl.ds(z, 1), :], (8, 128)) for comp in range(3)]
                for t in targets
            ]
            if n == 0:
                init = tuple(jnp.zeros((8, 128), jnp.float32) for _ in range(4 * len(targets)))
            else:
                init = tuple(near[comp, t, z] for t in targets for comp in range(4))

            def body(it, sums):
                sums = list(sums)
                granule = first + it * unroll
                rows = table[
                    pl.ds(pl.multiple_of(list_base[n] + granule * 8, 8), 8 * unroll), :
                ]
                for u in range(unroll):
                    piece = rows[8 * u : 8 * u + 8]
                    xs, ys, zs, cs = (
                        jnp.broadcast_to(piece[:, k : k + 1], (8, 128)) for k in (0, 16, 32, 48)
                    )
                    cs = jnp.where(granule + u < last, cs, 0.0)
                    for k in range(len(targets)):
                        dx = at[k][0] - xs
                        dy = at[k][1] - ys
                        dz = at[k][2] - zs
                        inverse = lax.rsqrt(dx * dx + dy * dy + (dz * dz + SOFTENING))
                        weight = cs * inverse
                        cubed = weight * (inverse * inverse)
                        sums[4 * k] += weight
                        sums[4 * k + 1] += cubed * dx
                        sums[4 * k + 2] += cubed * dy
                        sums[4 * k + 3] += cubed * dz
                return tuple(sums)

            sums = lax.fori_loop(0, (last - first + unroll - 1) // unroll, body, init)
            for k, t in enumerate(targets):
                for comp in range(4):
                    near[comp, t, z] = sums[4 * k + comp]
        return carry

    lax.fori_loop(0, 16, step, 0)


def stack_multipoles(mg, padded, stacked):
    cell = lax.broadcasted_iota(jnp.int32, (8, 128), 0)
    lane = lax.broadcasted_iota(jnp.int32, (8, 128), 1)
    padded[...] = jnp.zeros(padded.shape, jnp.float32)
    for s in range(SLOTS):
        padded[s, 8:16, :] = mg[s]
    even = cell % 2 == 0
    current = jnp.zeros((8, 128), jnp.float32)
    for k, (a, b, c) in enumerate(far_offsets):
        value = padded[(a + REACH) * WIDTH + b + REACH, 8 + c : 16 + c, :]
        if c == 3:
            value = jnp.where(even, value, 0.0)
        elif c == -3:
            value = jnp.where(even, 0.0, value)
        tile, shift = divmod(k * COEF, 128)
        rolled = pltpu.roll(value, shift, 1) if shift else value
        current = jnp.where(lane >= shift, rolled, current)
        if shift + COEF >= 128:
            stacked[:, tile * 128 : tile * 128 + 128] = current
            current = rolled
    last = CLASSES * COEF
    tile, shift = divmod(last, 128)
    if shift:
        stacked[:, tile * 128 : tile * 128 + 128] = jnp.where(lane < shift, current, 0.0)


CHUNK = 4096


def local_expansion(stacked, operator):
    total = jnp.zeros((8, COEF), jnp.float32)
    width = CLASSES * COEF
    for start in range(0, width, CHUNK):
        stop = min(start + CHUNK, width)
        total += lax.dot_general(
            stacked[:, start:stop].astype(jnp.bfloat16),
            operator[:, start:stop],
            (((1,), (1,)), ((), ())),
            preferred_element_type=jnp.float32,
        )
    return total


def far_tables(local, coefs):
    def factor(degree, moment):
        if degree > ORDER or moment > degree:
            return None
        scale = scale_of(degree, moment)
        pick = lambda index: jnp.broadcast_to(local[:, index : index + 1], (8, 128)) * scale
        real = pick(coef_index(degree, moment))
        imag = -pick(coef_index(degree, moment, 1)) if moment else None
        return real, imag

    zero = jnp.zeros((8, 128), jnp.float32)
    index = 0
    for moment in range(ORDER + 1):
        for degree in range(moment, ORDER + 1):
            own = factor(degree, moment)
            coefs[0, index, 0] = own[0]
            if moment:
                coefs[0, index, 1] = own[1]
            if degree < ORDER:
                below = factor(degree + 1, moment - 1) if moment else None
                above = factor(degree + 1, moment + 1)
                level = factor(degree + 1, moment)
                weight = 1.0 if moment == 1 else 0.5
                low = (zero, zero)
                if below:
                    low = (weight * below[0], zero if below[1] is None else weight * below[1])
                high = (0.5 * above[0], 0.5 * above[1])
                coefs[1, index, 0] = low[0] - high[0]
                coefs[2, index, 0] = low[1] + high[1]
                coefs[3, index, 0] = level[0]
                if moment:
                    coefs[1, index, 1] = low[1] - high[1]
                    coefs[2, index, 1] = -(low[0] + high[0])
                    coefs[3, index, 1] = level[1]
            index += 1


def finish(tab, near, coefs, pot_ref, field_ref):
    i = lax.axis_index("gx")
    j = lax.axis_index("gy")
    cell = lax.broadcasted_iota(jnp.int32, (8, 128), 0).astype(jnp.float32)
    self_term = lax.rsqrt(jnp.full((8, 128), SOFTENING, jnp.float32))
    for bz in range(2):
        rows = pl.ds(bz, 8, stride=2)
        pick = lambda comp: jnp.stack([tab[t, comp, rows, :] for t in own_columns])
        x = pick(0) - (2 * i + 1).astype(jnp.float32)
        y = pick(1) - (2 * j + 1).astype(jnp.float32)
        z = pick(2) - (2.0 * cell + 1.0)[None]
        sums = [jnp.zeros((4, 8, 128), jnp.float32) for _ in range(4)]
        index = 0
        for degree, moment, real, imag in harmonic_columns(x, y, z, ORDER):
            for out in range(4 if degree < ORDER else 1):
                sums[out] += coefs[out, index, 0][None] * real
                if moment:
                    sums[out] -= coefs[out, index, 1][None] * imag
            index += 1
        for k, t in enumerate(own_columns):
            leaf = (t // 4 - 1) + 2 * (t % 4 - 1) + 4 * bz
            dest = pl.ds(leaf, 8, stride=8)
            pair = [near[comp, t, rows] for comp in range(4)]
            close = [jnp.sum(v, axis=1) for v in pair]
            charge = tab[t, 3, rows, :]
            pot_ref[dest, :] = sums[0][k] + (close[0] - charge * self_term)
            for comp in range(3):
                field_ref[comp, dest, :] = close[comp + 1] - sums[comp + 1][k]


def evaluate_kernel(
    cnt, tab, mg, translations, pot_ref, field_ref,
    columns, table, starts, near, padded, stacked, operator, coefs, copy_sem,
):
    fetch = pltpu.make_async_copy(translations, operator, copy_sem)
    fetch.start()
    build_sources(tab, cnt, columns, table, starts)
    near_field(tab, table, starts, near)
    stack_multipoles(mg, padded, stacked)
    fetch.wait()
    local = local_expansion(stacked, operator)
    far_tables(local, coefs)
    finish(tab, near, coefs, pot_ref, field_ref)


def evaluate(cnt, tab, mg, translations):
    vmem = pl.BlockSpec(memory_space=pltpu.VMEM)
    f32 = jnp.float32
    return pl.pallas_call(
        evaluate_kernel,
        out_shape=(
            jax.ShapeDtypeStruct((64, 128), f32),
            jax.ShapeDtypeStruct((3, 64, 128), f32),
        ),
        in_specs=[
            pl.BlockSpec(memory_space=pltpu.SMEM),
            vmem,
            vmem,
            pl.BlockSpec(memory_space=pl.ANY),
        ],
        out_specs=(vmem, vmem),
        scratch_shapes=[
            pltpu.VMEM((16, 128, 128), f32),
            pltpu.VMEM((TABLE_ROWS, 128), f32),
            pltpu.SMEM((len(source_lists), 17), jnp.int32),
            pltpu.VMEM((4, 16, 16, 8, 128), f32),
            pltpu.VMEM((SLOTS, 24, 128), f32),
            pltpu.VMEM((8, TILES * 128), f32),
            pltpu.VMEM((COEF, CLASSES * COEF), jnp.bfloat16),
            pltpu.VMEM((4, 66, 2, 8, 128), f32),
            pltpu.SemaphoreType.DMA,
        ],
        compiler_params=pltpu.CompilerParams(vmem_limit_bytes=56 << 20),
        name="evaluate",
    )(cnt, tab, mg, translations)


def per_device(
    positions, charges, send_x, send_y, send_corner, near_slot, far_sources, translations
):
    tab, mg, cnt = exchange(jnp.transpose(positions, (1, 0, 2)), charges)
    potential, field = evaluate(cnt, tab, mg, translations)
    return potential, jnp.transpose(field, (1, 0, 2))


def solution(mesh):
    return jax.shard_map(
        per_device,
        mesh=mesh,
        in_specs=(
            P(("gx", "gy"), None, None),
            P(("gx", "gy"), None),
            P(("gx", "gy"), None, None),
            P(("gx", "gy"), None, None),
            P(("gx", "gy"), None, None),
            P(("gx", "gy"), None),
            P(("gx", "gy"), None),
            P(),
        ),
        out_specs=(P(("gx", "gy"), None), P(("gx", "gy"), None, None)),
        check_vma=False,
    )
```

time: 875 us -> 168 us (0.19)
  the two profiles are of different devices: /device:TPU:69 before, /device:TPU:99 now
where the time goes in v1:
time: 168 us; the launch traced here: 167 us
  Pallas kernels  150 us (89%)
  local copies, waits for them, and re-layouts  16.9 us (10%)
    pallas_call x1, Pallas kernels, evaluate(): pl.pallas_call(evaluate_kernel, out_shape=(jax.ShapeDtypeStruct((64, 128)...  137 us
    unnamed x11, local copies, waits for them, and re-layouts  16.9 us
    pallas_call x1, Pallas kernels, exchange(): pl.pallas_call(exchange_kernel, out_shape=(jax.ShapeDtypeStruct((16, 4, 1...  13.3 us

profile of v1, /device:TPU:99, one launch (start us, length us, event | category | flops | bytes accessed | tf_op | source)
XLA Modules:
  0.0 167.4 jit_solution(13688418510748424210)
XLA Ops:
  0.6 0.0 copy-start.2
  0.6 0.9 copy-done.2
  1.5 0.0 copy-start.3
  1.5 0.8 copy-done.3
  2.3 13.3 %exchange.1 = (f32[16,4,16,128]{3,2,1,0:T(8,128)S(1)}, f32[49,8,128]{2,1,0:T(8,128)S(1)}, s32[16,128]{1,0:T(8,128)S(1)}) custom-call(f32[3,64,128]{2,1,0:T(8,128)S(1)} %bitcast.2, f32[64,128]{1,0:T(8,128)S(1)} %copy-done.3), custom_call_target="tpu_custom_call" | custom-call | tf_op jit(solution)/shard_map/exchange/pallas_call | solution.py:215
  15.6 0.0 copy-start
  15.6 0.8 copy-done
  16.4 0.0 copy-start.1
  16.4 0.7 copy-done.1
  17.1 0.0 copy-start.4
  17.1 0.6 copy-done.4
  17.7 13.2 %copy.5.translations = bf16[121,38236]{1,0:T(8,128)(2,1)} copy(bf16[121,38236]{0,1:T(8,128)(2,1)} %param.10) | data formatting | bytes 18506224 | tf_op args[7]
  30.9 136.5 %evaluate.1 = (f32[64,128]{1,0:T(8,128)}, f32[3,64,128]{2,1,0:T(8,128)}) custom-call(s32[16,128]{1,0:T(8,128)} %copy-done.4, f32[16,4,16,128]{3,2,1,0:T(8,128)} %copy-done, f32[49,8,128]{2,1,0:T(8,128)} %copy-done.1, bf16[121,38236]{1,0:T(8,128)(2,1)} %copy.5.translations), custom_call_target="tpu_custom_call" | custom-call | tf_op jit(solution)/shard_map/evaluate/pallas_call | solution.py:454
Async XLA Ops:
  0.6 0.9 copy-start.2
  1.5 0.8 copy-start.3
  15.6 0.8 copy-start
  16.4 0.7 copy-start.1
  17.1 0.6 copy-start.4

commit v2 on v1

--- a/solution.py
+++ b/solution.py
@@ -246,81 +246,99 @@
     ((15,), (10,)),
 ]
 own_columns = (5, 6, 9, 10)
-unrolls = {4: 4, 2: 8, 1: 8}
-list_rows = [(len(sources) * 16 + 1) * 128 for sources, _ in source_lists]
-list_base = [sum(list_rows[:n]) for n in range(len(list_rows))]
-TABLE_ROWS = sum(list_rows)
-
-
-def build_sources(tab, cnt, columns, table, starts):
-    for column in range(16):
+unrolls = {4: 8, 2: 8, 1: 8}
+ring_slots = [4 * 16 * len(sources) for sources, _ in source_lists]
+ring_base = [sum(ring_slots[:n]) for n in range(len(ring_slots))]
+RING = sum(ring_slots)
+
+
+def build_sources(cnt, columns, starts, ring, z):
+    row = lax.broadcasted_iota(jnp.int32, (256, 512), 0)
+    comp_of = lax.broadcasted_iota(jnp.int32, (256, 512), 1) // 128
+    pick = ((row % 64 == comp_of * 16 + z) & (row < 192)).astype(jnp.float32).astype(jnp.bfloat16)
+    for n, (sources, _) in enumerate(source_lists):
+        base = sum(len(s) for s, _ in source_lists[:n]) * 128
+        spread = jnp.dot(
+            columns[base : base + 128 * len(sources), :], pick, preferred_element_type=jnp.float32
+        )
+        offset = starts[n, z]
+        for k, column in enumerate(sources):
+            for g in range(16):
+                slot = ring_base[n] + ((offset + g) & (ring_slots[n] - 1))
+                rows = slice(128 * k + 8 * g, 128 * k + 8 * g + 8)
+                for comp in range(4):
+                    ring[slot, comp] = spread[rows, 128 * comp : 128 * comp + 128]
+            offset = offset + (cnt[z, column] + 7) // 8
+        starts[n, z + 1] = offset
+
+
+def near_slab(tab, starts, ring, near, z):
+    for n, (_, targets) in enumerate(source_lists):
+        unroll = unrolls[len(targets)]
+        first = starts[n, jnp.maximum(z - 1, 0)]
+        last = starts[n, jnp.minimum(z + 2, 16)]
+        at = [
+            [jnp.broadcast_to(tab[t, comp, pl.ds(z, 1), :], (8, 128)) for comp in range(3)]
+            for t in targets
+        ]
+        if n == 0:
+            init = tuple(jnp.zeros((8, 128), jnp.float32) for _ in range(4 * len(targets)))
+        else:
+            init = tuple(near[comp, t, z] for t in targets for comp in range(4))
+
+        def body(it, sums):
+            sums = list(sums)
+            for u in range(unroll):
+                granule = first + it * unroll + u
+                slot = ring_base[n] + (jnp.minimum(granule, last - 1) & (ring_slots[n] - 1))
+                xs, ys, zs, cs = (ring[slot, comp] for comp in range(4))
+                cs = jnp.where(granule < last, cs, 0.0)
+                for k in range(len(targets)):
+                    dx = at[k][0] - xs
+                    dy = at[k][1] - ys
+                    dz = at[k][2] - zs
+                    inverse = lax.rsqrt(dx * dx + dy * dy + (dz * dz + SOFTENING))
+                    weight = cs * inverse
+                    cubed = weight * (inverse * inverse)
+                    sums[4 * k] += weight
+                    sums[4 * k + 1] += cubed * dx
+                    sums[4 * k + 2] += cubed * dy
+                    sums[4 * k + 3] += cubed * dz
+            return tuple(sums)
+
+        sums = lax.fori_loop(0, (last - first + unroll - 1) // unroll, body, init)
+        for k, t in enumerate(targets):
+            for comp in range(4):
+                near[comp, t, z] = sums[4 * k + comp]
+
+
+def near_field(tab, cnt, columns, starts, ring, near):
+    low_lanes = lax.broadcasted_iota(jnp.int32, (128, 128), 1) < 64
+    order = [column for sources, _ in source_lists for column in sources]
+    for place, column in enumerate(order):
         flat = tab[column].reshape(64, 128)
-        columns[column] = jnp.transpose(jnp.concatenate([flat, flat], axis=0))
-
-    def step(z, offsets):
-        offsets = list(offsets)
-        for n, (sources, _) in enumerate(source_lists):
-            starts[n, z] = offsets[n]
-            for column in sources:
-                rows = pl.ds(pl.multiple_of(list_base[n] + offsets[n] * 8, 8), 128)
-                table[rows, :] = pltpu.roll(columns[column], (128 - z) % 128, 1)
-                offsets[n] = offsets[n] + (cnt[z, column] + 7) // 8
-        return tuple(offsets)
-
-    ends = lax.fori_loop(0, 16, step, (jnp.int32(0),) * len(source_lists))
-    for n, end in enumerate(ends):
-        starts[n, 16] = end
-        rows = pl.ds(pl.multiple_of(list_base[n] + end * 8, 8), 128)
-        table[rows, :] = jnp.zeros((128, 128), jnp.float32)
-
-
-def near_field(tab, table, starts, near):
+        value = jnp.transpose(jnp.concatenate([flat, flat], axis=0))
+        high = value.astype(jnp.bfloat16).astype(jnp.float32)
+        rest = value - high
+        middle = rest.astype(jnp.bfloat16).astype(jnp.float32)
+        rows = slice(128 * place, 128 * place + 128)
+        columns[rows, :128] = jnp.where(low_lanes, high, middle).astype(jnp.bfloat16)
+        columns[rows, 128:] = jnp.where(low_lanes, rest - middle, 0.0).astype(jnp.bfloat16)
+    for n in range(len(source_lists)):
+        starts[n, 0] = 0
+
     def step(z, carry):
-        for n, (_, targets) in enumerate(source_lists):
-            unroll = unrolls[len(targets)]
-            first = starts[n, jnp.maximum(z - 1, 0)]
-            last = starts[n, jnp.minimum(z + 2, 16)]
-            at = [
-                [jnp.broadcast_to(tab[t, comp, pl.ds(z, 1), :], (8, 128)) for comp in range(3)]
-                for t in targets
-            ]
-            if n == 0:
-                init = tuple(jnp.zeros((8, 128), jnp.float32) for _ in range(4 * len(targets)))
-            else:
-                init = tuple(near[comp, t, z] for t in targets for comp in range(4))
-
-            def body(it, sums):
-                sums = list(sums)
-                granule = first + it * unroll
-                rows = table[
-                    pl.ds(pl.multiple_of(list_base[n] + granule * 8, 8), 8 * unroll), :
-                ]
-                for u in range(unroll):
-                    piece = rows[8 * u : 8 * u + 8]
-                    xs, ys, zs, cs = (
-                        jnp.broadcast_to(piece[:, k : k + 1], (8, 128)) for k in (0, 16, 32, 48)
-                    )
-                    cs = jnp.where(granule + u < last, cs, 0.0)
-                    for k in range(len(targets)):
-                        dx = at[k][0] - xs
-                        dy = at[k][1] - ys
-                        dz = at[k][2] - zs
-                        inverse = lax.rsqrt(dx * dx + dy * dy + (dz * dz + SOFTENING))
-                        weight = cs * inverse
-                        cubed = weight * (inverse * inverse)
-                        sums[4 * k] += weight
-                        sums[4 * k + 1] += cubed * dx
-                        sums[4 * k + 2] += cubed * dy
-                        sums[4 * k + 3] += cubed * dz
-                return tuple(sums)
-
-            sums = lax.fori_loop(0, (last - first + unroll - 1) // unroll, body, init)
-            for k, t in enumerate(targets):
-                for comp in range(4):
-                    near[comp, t, z] = sums[4 * k + comp]
+        @pl.when(z < 16)
+        def _():
+            build_sources(cnt, columns, starts, ring, z)
+
+        @pl.when(z > 0)
+        def _():
+            near_slab(tab, starts, ring, near, z - 1)
+
         return carry
 
-    lax.fori_loop(0, 16, step, 0)
+    lax.fori_loop(0, 17, step, 0)
 
 
 def stack_multipoles(mg, padded, stacked):
@@ -359,8 +377,8 @@
         stop = min(start + CHUNK, width)
         total += lax.dot_general(
             stacked[:, start:stop].astype(jnp.bfloat16),
-            operator[:, start:stop],
-            (((1,), (1,)), ((), ())),
+            operator[start:stop, :],
+            (((1,), (0,)), ((), ())),
             preferred_element_type=jnp.float32,
         )
     return total
@@ -435,12 +453,11 @@
 
 def evaluate_kernel(
     cnt, tab, mg, translations, pot_ref, field_ref,
-    columns, table, starts, near, padded, stacked, operator, coefs, copy_sem,
+    columns, starts, ring, near, padded, stacked, operator, coefs, copy_sem,
 ):
     fetch = pltpu.make_async_copy(translations, operator, copy_sem)
     fetch.start()
-    build_sources(tab, cnt, columns, table, starts)
-    near_field(tab, table, starts, near)
+    near_field(tab, cnt, columns, starts, ring, near)
     stack_multipoles(mg, padded, stacked)
     fetch.wait()
     local = local_expansion(stacked, operator)
@@ -465,17 +482,17 @@
         ],
         out_specs=(vmem, vmem),
         scratch_shapes=[
-            pltpu.VMEM((16, 128, 128), f32),
-            pltpu.VMEM((TABLE_ROWS, 128), f32),
+            pltpu.VMEM((2048, 256), jnp.bfloat16),
             pltpu.SMEM((len(source_lists), 17), jnp.int32),
+            pltpu.VMEM((RING, 4, 8, 128), f32),
             pltpu.VMEM((4, 16, 16, 8, 128), f32),
             pltpu.VMEM((SLOTS, 24, 128), f32),
             pltpu.VMEM((8, TILES * 128), f32),
-            pltpu.VMEM((COEF, CLASSES * COEF), jnp.bfloat16),
+            pltpu.VMEM((CLASSES * COEF, COEF), jnp.bfloat16),
             pltpu.VMEM((4, 66, 2, 8, 128), f32),
             pltpu.SemaphoreType.DMA,
         ],
-        compiler_params=pltpu.CompilerParams(vmem_limit_bytes=56 << 20),
+        compiler_params=pltpu.CompilerParams(vmem_limit_bytes=58 << 20),
         name="evaluate",
     )(cnt, tab, mg, translations)
 
@@ -484,7 +501,7 @@
     positions, charges, send_x, send_y, send_corner, near_slot, far_sources, translations
 ):
     tab, mg, cnt = exchange(jnp.transpose(positions, (1, 0, 2)), charges)
-    potential, field = evaluate(cnt, tab, mg, translations)
+    potential, field = evaluate(cnt, tab, mg, jnp.transpose(translations))
     return potential, jnp.transpose(field, (1, 0, 2))
 
 

time: 168 us -> 84.8 us (0.50)
  the two profiles are of different devices: /device:TPU:99 before, /device:TPU:69 now
where the time goes in v2:
time: 84.8 us; the launch traced here: 84.6 us
  Pallas kernels  80.3 us (95%)
  local copies, waits for them, and re-layouts  3.69 us (4%)
    pallas_call x1, Pallas kernels, evaluate(): pl.pallas_call(evaluate_kernel, out_shape=(jax.ShapeDtypeStruct((64, 128)...  66.8 us
    pallas_call x1, Pallas kernels, exchange(): pl.pallas_call(exchange_kernel, out_shape=(jax.ShapeDtypeStruct((16, 4, 1...  13.5 us
    unnamed x10, local copies, waits for them, and re-layouts  3.69 us

profile of v2, /device:TPU:69, one launch (start us, length us, event | category | flops | bytes accessed | tf_op | source)
XLA Modules:
  0.0 84.6 jit_solution(710292086203886315)
XLA Ops:
  0.6 0.0 copy-start.2
  0.6 0.9 %copy-done.2 = f32[64,3,128]{2,0,1:T(8,128)S(1)} copy-done((f32[64,3,128]{2,0,1:T(8,128)S(1)}, f32[64,3,128]{2,0,1:T(8,128)}, u32[]{:S(2)}) %copy-start.2) | copy-done | bytes 98328
  1.5 0.0 copy-start.3
  1.5 0.8 copy-done.3
  2.3 13.5 %exchange.1 = (f32[16,4,16,128]{3,2,1,0:T(8,128)S(1)}, f32[49,8,128]{2,1,0:T(8,128)S(1)}, s32[16,128]{1,0:T(8,128)S(1)}) custom-call(f32[3,64,128]{2,1,0:T(8,128)S(1)} %bitcast.3, f32[64,128]{1,0:T(8,128)S(1)} %copy-done.3), custom_call_target="tpu_custom_call" | custom-call | tf_op jit(solution)/shard_map/exchange/pallas_call | solution.py:215
  15.8 0.0 copy-start
  15.8 0.8 copy-done
  16.6 0.0 copy-start.1
  16.6 0.7 copy-done.1
  17.3 0.0 copy-start.4
  17.3 0.6 copy-done.4
  17.9 66.8 %evaluate.1 = (f32[64,128]{1,0:T(8,128)}, f32[3,64,128]{2,1,0:T(8,128)}) custom-call(s32[16,128]{1,0:T(8,128)} %copy-done.4, f32[16,4,16,128]{3,2,1,0:T(8,128)} %copy-done, f32[49,8,128]{2,1,0:T(8,128)} %copy-done.1, bf16[38236,121]{1,0:T(8,128)(2,1)} %bitcast.4), custom_call_target="tpu_custom_call" | custom-call | tf_op jit(solution)/shard_map/evaluate/pallas_call | solution.py:471
Async XLA Ops:
  0.6 0.9 %copy-start.2 = (f32[64,3,128]{2,0,1:T(8,128)S(1)}, f32[64,3,128]{2,0,1:T(8,128)}, u32[]{:S(2)}) copy-start(f32[64,3,128]{2,0,1:T(8,128)} %param.8) | copy-start | bytes 294916
  1.5 0.8 copy-start.3
  15.8 0.8 copy-start
  16.6 0.7 copy-start.1
  17.3 0.6 copy-start.4

commit v3 on v2

--- a/solution.py
+++ b/solution.py
@@ -79,10 +79,19 @@
 )
 
 
-def exchange_kernel(pos_ref, charge_ref, tab, mg, cnt, send_m, recv_m, send_h, recv_h):
+def exchange_kernel(
+    pos_any, charge_any, tab, mg, cnt,
+    pos_ref, charge_ref, fetch_sem, send_m, recv_m, send_h, recv_h,
+):
     i = lax.axis_index("gx")
     j = lax.axis_index("gy")
     zero_tile = jnp.zeros((8, 128), jnp.float32)
+    fetches = [
+        pltpu.make_async_copy(pos_any, pos_ref, fetch_sem.at[0]),
+        pltpu.make_async_copy(charge_any, charge_ref, fetch_sem.at[1]),
+    ]
+    for fetch in fetches:
+        fetch.start()
     mg[...] = jnp.zeros(mg.shape, jnp.float32)
     for column in range(16):
         if column not in (5, 6, 9, 10):
@@ -100,6 +109,8 @@
         return count + ok.astype(jnp.int32)
 
     total = lax.fori_loop(0, 24, signal_partner, jnp.int32(0))
+    for fetch in fetches:
+        fetch.wait()
     for bx in range(2):
         for by in range(2):
             column = 4 * (1 + bx) + 1 + by
@@ -219,16 +230,19 @@
             jax.ShapeDtypeStruct((SLOTS, 8, 128), jnp.float32),
             jax.ShapeDtypeStruct((16, 128), jnp.int32),
         ),
-        in_specs=[vmem, vmem],
+        in_specs=[pl.BlockSpec(memory_space=pltpu.HBM)] * 2,
         out_specs=(vmem, vmem, vmem),
         scratch_shapes=[
+            pltpu.VMEM((3, 64, 128), jnp.float32),
+            pltpu.VMEM((64, 128), jnp.float32),
+            pltpu.SemaphoreType.DMA((2,)),
             pltpu.SemaphoreType.DMA((SLOTS,)),
             pltpu.SemaphoreType.DMA((SLOTS,)),
             pltpu.SemaphoreType.DMA((len(halo_moves),)),
             pltpu.SemaphoreType.DMA((len(halo_moves),)),
         ],
         compiler_params=pltpu.CompilerParams(
-            collective_id=0, has_side_effects=True, vmem_limit_bytes=40 << 20
+            collective_id=0, has_side_effects=True, vmem_limit_bytes=16 << 20
         ),
         name="exchange",
     )(pos, charges)
@@ -247,6 +261,7 @@
 ]
 own_columns = (5, 6, 9, 10)
 unrolls = {4: 8, 2: 8, 1: 8}
+depths = {4: 1, 2: 1, 1: 2}
 ring_slots = [4 * 16 * len(sources) for sources, _ in source_lists]
 ring_base = [sum(ring_slots[:n]) for n in range(len(ring_slots))]
 RING = sum(ring_slots)
@@ -286,27 +301,34 @@
         else:
             init = tuple(near[comp, t, z] for t in targets for comp in range(4))
 
-        def body(it, sums):
-            sums = list(sums)
+        def front(granule):
+            slot = ring_base[n] + (jnp.minimum(granule, last - 1) & (ring_slots[n] - 1))
+            xs, ys, zs, cs = (ring[slot, comp] for comp in range(4))
+            made = [jnp.where(granule < last, cs, 0.0)]
+            for x, y, z in at:
+                dx, dy, dz = x - xs, y - ys, z - zs
+                made += [dx, dy, dz, dx * dx + dy * dy + (dz * dz + SOFTENING)]
+            return made
+
+        def body(it, carry):
+            sums, queue = list(carry[0]), list(carry[1])
             for u in range(unroll):
-                granule = first + it * unroll + u
-                slot = ring_base[n] + (jnp.minimum(granule, last - 1) & (ring_slots[n] - 1))
-                xs, ys, zs, cs = (ring[slot, comp] for comp in range(4))
-                cs = jnp.where(granule < last, cs, 0.0)
+                queue.append(front(first + depth + it * unroll + u))
+                cs, *parts = queue.pop(0)
                 for k in range(len(targets)):
-                    dx = at[k][0] - xs
-                    dy = at[k][1] - ys
-                    dz = at[k][2] - zs
-                    inverse = lax.rsqrt(dx * dx + dy * dy + (dz * dz + SOFTENING))
+                    dx, dy, dz, square = parts[4 * k : 4 * k + 4]
+                    inverse = lax.rsqrt(square)
                     weight = cs * inverse
                     cubed = weight * (inverse * inverse)
                     sums[4 * k] += weight
                     sums[4 * k + 1] += cubed * dx
                     sums[4 * k + 2] += cubed * dy
                     sums[4 * k + 3] += cubed * dz
-            return tuple(sums)
-
-        sums = lax.fori_loop(0, (last - first + unroll - 1) // unroll, body, init)
+            return tuple(sums), queue
+
+        depth = depths[len(targets)]
+        queue = [front(first + u) for u in range(depth)]
+        sums = lax.fori_loop(0, (last - first + unroll - 1) // unroll, body, (init, queue))[0]
         for k, t in enumerate(targets):
             for comp in range(4):
                 near[comp, t, z] = sums[4 * k + comp]
@@ -492,7 +514,7 @@
             pltpu.VMEM((4, 66, 2, 8, 128), f32),
             pltpu.SemaphoreType.DMA,
         ],
-        compiler_params=pltpu.CompilerParams(vmem_limit_bytes=58 << 20),
+        compiler_params=pltpu.CompilerParams(vmem_limit_bytes=50 << 20),
         name="evaluate",
     )(cnt, tab, mg, translations)
 

time: 84.8 us -> 82.9 us (0.978)
  the two profiles are of different devices: /device:TPU:69 before, /device:TPU:27 now
where the time goes in v3:
time: 82.9 us; the launch traced here: 82.7 us
  Pallas kernels  80.4 us (97%)
  local copies, waits for them, and re-layouts  1.64 us (2%)
    pallas_call x1, Pallas kernels, evaluate(): pl.pallas_call(evaluate_kernel, out_shape=(jax.ShapeDtypeStruct((64, 128)...  67.1 us
    pallas_call x1, Pallas kernels, exchange(): pl.pallas_call(exchange_kernel, out_shape=(jax.ShapeDtypeStruct((16, 4, 1...  13.3 us

profile of v3, /device:TPU:27, one launch (start us, length us, event | category | flops | bytes accessed | tf_op | source)
XLA Modules:
  0.0 82.7 jit_solution(645691192650184760)
XLA Ops:
  0.6 0.0 copy-start
  0.6 0.9 %copy-done = f32[64,3,128]{2,0,1:T(8,128)S(1)} copy-done((f32[64,3,128]{2,0,1:T(8,128)S(1)}, f32[64,3,128]{2,0,1:T(8,128)}, u32[]{:S(2)}) %copy-start) | copy-done | bytes 98328
  1.5 0.0 copy-start.1
  1.5 0.8 copy-done.1
  2.3 13.3 %exchange.1 = (f32[16,4,16,128]{3,2,1,0:T(8,128)S(1)}, f32[49,8,128]{2,1,0:T(8,128)S(1)}, s32[16,128]{1,0:T(8,128)S(1)}) custom-call(f32[3,64,128]{2,1,0:T(8,128)S(1)} %bitcast.3, f32[64,128]{1,0:T(8,128)S(1)} %copy-done.1), custom_call_target="tpu_custom_call" | custom-call | tf_op jit(solution)/shard_map/exchange/pallas_call | solution.py:226
  15.6 67.1 %evaluate.1 = (f32[64,128]{1,0:T(8,128)}, f32[3,64,128]{2,1,0:T(8,128)}) custom-call(s32[16,128]{1,0:T(8,128)S(1)} %get-tuple-element.7.cnt, f32[16,4,16,128]{3,2,1,0:T(8,128)S(1)} %get-tuple-element.8.tab, f32[49,8,128]{2,1,0:T(8,128)S(1)} %get-tuple-element.9.mg, bf16[38236,121]{1,0:T(8,128)(2,1)} %bitcast.4), custom_call_target="tpu_custom_call" | custom-call | tf_op jit(solution)/shard_map/evaluate/pallas_call | solution.py:493
Async XLA Ops:
  0.6 0.9 %copy-start = (f32[64,3,128]{2,0,1:T(8,128)S(1)}, f32[64,3,128]{2,0,1:T(8,128)}, u32[]{:S(2)}) copy-start(f32[64,3,128]{2,0,1:T(8,128)} %param.8) | copy-start | bytes 294916
  1.5 0.8 copy-start.1

commit v4 on v3

--- a/solution.py
+++ b/solution.py
@@ -120,7 +120,6 @@
                 for comp in range(3):
                     tab[column, comp, dest, :] = pos_ref[comp, rows, :]
                 tab[column, 3, dest, :] = charge_ref[rows, :]
-    pl.semaphore_wait(barrier, total)
 
     def halo_copy(move, index):
         (da, db), source, dest = move
@@ -135,12 +134,6 @@
 
     def inside(a, b):
         return (i + a >= 0) & (i + a < GX) & (j + b >= 0) & (j + b < GY)
-
-    for index, move in enumerate(halo_moves):
-
-        @pl.when(inside(*move[0]))
-        def _():
-            halo_copy(move, index).start()
 
     cell = lax.broadcasted_iota(jnp.int32, (8, 128), 0).astype(jnp.float32)
     lane = lax.broadcasted_iota(jnp.int32, (8, 128), 1)
@@ -160,6 +153,7 @@
             index = coef_index(degree, moment, part)
             moments = jnp.where(lane == index, scale_of(degree, moment) * summed, moments)
     mg[OWN] = moments.astype(jnp.bfloat16).astype(jnp.float32)
+    pl.semaphore_wait(barrier, total)
 
     def multipole_copy(pi, pj):
         there = (i - pi + REACH) * WIDTH + (j - pj + REACH)
@@ -182,6 +176,12 @@
         return carry
 
     lax.fori_loop(0, 24, send_multipole, 0)
+
+    for index, move in enumerate(halo_moves):
+
+        @pl.when(inside(*move[0]))
+        def _():
+            halo_copy(move, index).start()
 
     def wait_multipole(t, carry):
         pi, pj, ok = partners(i, j, t)

time: 82.9 us -> 84.6 us (1.021)
  the two profiles are of different devices: /device:TPU:27 before, /device:TPU:69 now
where the time goes in v4:
time: 84.6 us; the launch traced here: 83.2 us
  Pallas kernels  80.9 us (96%)
  local copies, waits for them, and re-layouts  1.64 us (2%)
    pallas_call x1, Pallas kernels, evaluate(): pl.pallas_call(evaluate_kernel, out_shape=(jax.ShapeDtypeStruct((64, 128)...  69.3 us
    pallas_call x1, Pallas kernels, exchange(): pl.pallas_call(exchange_kernel, out_shape=(jax.ShapeDtypeStruct((16, 4, 1...  11.6 us

profile of v4, /device:TPU:69, one launch (start us, length us, event | category | flops | bytes accessed | tf_op | source)
XLA Modules:
  0.0 83.2 jit_solution(17905561602862454276)
XLA Ops:
  0.6 0.0 copy-start
  0.6 0.9 %copy-done = f32[64,3,128]{2,0,1:T(8,128)S(1)} copy-done((f32[64,3,128]{2,0,1:T(8,128)S(1)}, f32[64,3,128]{2,0,1:T(8,128)}, u32[]{:S(2)}) %copy-start) | copy-done | bytes 98328
  1.5 0.0 copy-start.1
  1.5 0.8 copy-done.1
  2.3 11.6 %exchange.1 = (f32[16,4,16,128]{3,2,1,0:T(8,128)S(1)}, f32[49,8,128]{2,1,0:T(8,128)S(1)}, s32[16,128]{1,0:T(8,128)S(1)}) custom-call(f32[3,64,128]{2,1,0:T(8,128)S(1)} %bitcast.3, f32[64,128]{1,0:T(8,128)S(1)} %copy-done.1), custom_call_target="tpu_custom_call" | custom-call | tf_op jit(solution)/shard_map/exchange/pallas_call | solution.py:226
  13.9 69.3 %evaluate.1 = (f32[64,128]{1,0:T(8,128)}, f32[3,64,128]{2,1,0:T(8,128)}) custom-call(s32[16,128]{1,0:T(8,128)S(1)} %get-tuple-element.7.cnt, f32[16,4,16,128]{3,2,1,0:T(8,128)S(1)} %get-tuple-element.8.tab, f32[49,8,128]{2,1,0:T(8,128)S(1)} %get-tuple-element.9.mg, bf16[38236,121]{1,0:T(8,128)(2,1)} %bitcast.4), custom_call_target="tpu_custom_call" | custom-call | tf_op jit(solution)/shard_map/evaluate/pallas_call | solution.py:493
Async XLA Ops:
  0.6 0.9 %copy-start = (f32[64,3,128]{2,0,1:T(8,128)S(1)}, f32[64,3,128]{2,0,1:T(8,128)}, u32[]{:S(2)}) copy-start(f32[64,3,128]{2,0,1:T(8,128)} %param.8) | copy-start | bytes 294916
  1.5 0.8 copy-start.1
